TPU v7x, 32 devices: a whole 2x2x4 slice. The times are simulated.
32 devices in a mesh: gx: 4 (over y, x), gy: 8 (over z, core).
Axes of the slice: x: 2, y: 2, z: 4, core: 2. Of those that a mesh axis runs over, the one named last changes fastest.
Arguments:
- picture_embeds: bfloat16 [32768, 1152], P(('gx', 'gy')), may hold values from -6 to 6
- motion_embeds: bfloat16 [32768, 1152], P(('gx', 'gy')), may hold values from -6 to 6
- match_indices: int32 [32, 1024], P(('gx', 'gy')), may hold values from 0 to 1023, each once within a row
- sharpness_coefficient: float32 [1], replicated, may hold values from 0.04 to 0.12
- additive_shift: float32 [1], replicated, may hold values from -3 to -1
- precision_gain: float32 [1], replicated, may hold values from 16384 to 65536
Outputs:
- grad_image: bfloat16 [32768, 1152], P(('gx', 'gy'))
- grad_sensor: bfloat16 [32768, 1152], P(('gx', 'gy'))
Inputs may be any that keep to these rules, and one draw needn't show every extreme that they name: Each row of match_indices is a permutation of 0 to 1023.
All inputs are finite; a program needn't handle non-finite values.
Results may differ from a plain program's by a relative error of at most 0.0038.
Values may be sent and summed in bfloat16 or wider, within the bound.
A program may use at most 128 MiB of HBM per device.

v0:
```python
import jax
import jax.numpy as jnp
from jax import lax
from jax.sharding import PartitionSpec as P


def shifted(value, axis, by):
    devices = lax.axis_size(axis)
    return lax.ppermute(value, axis, [(i, (i + by) % devices) for i in range(devices)])


def pairing_weights(
    western_entries,
    eastern_entries,
    sharpness_coefficient,
    additive_shift,
    objective_coefficient,
    match_target,
):
    similarity_grid = lax.dot_general(
        western_entries,
        eastern_entries,
        (((1,), (1,)), ((), ())),
        preferred_element_type=jnp.float32,
    )
    logistic_derivative = jax.nn.sigmoid(
        sharpness_coefficient[0] * similarity_grid + additive_shift[0]
    )
    if match_target is not None:
        logistic_derivative = logistic_derivative - match_target
    return (objective_coefficient * logistic_derivative).astype(jnp.bfloat16)


def apply_rows(weights, eastern_entries):
    return jnp.dot(weights, eastern_entries, preferred_element_type=jnp.float32)


def apply_cols(weights, western_entries):
    return lax.dot_general(
        weights, western_entries, (((0,), (0,)), ((), ())), preferred_element_type=jnp.float32
    )


def step_ahead(blockwise):
    return shifted(blockwise, ("gx", "gy"), -1)


def carry_ahead(carried):
    return shifted(carried, ("gx", "gy"), 1)


def per_device(
    picture_embeds,
    motion_embeds,
    match_indices,
    sharpness_coefficient,
    additive_shift,
    precision_gain,
):
    row_count = picture_embeds.shape[0]
    entire_height = row_count * lax.axis_size(("gx", "gy"))
    objective_coefficient = precision_gain[0] * sharpness_coefficient[0] / entire_height
    columns = jnp.arange(row_count, dtype=jnp.int32)
    match_target = (match_indices[0][:, None] == columns[None, :]).astype(jnp.float32)
    local_weights = pairing_weights(
        picture_embeds,
        motion_embeds,
        sharpness_coefficient,
        additive_shift,
        objective_coefficient,
        match_target,
    )
    grad_img = apply_rows(local_weights, motion_embeds)
    own_terms = apply_cols(local_weights, picture_embeds)
    motion_predecessor = shifted(motion_embeds, ("gx", "gy"), 1)
    motion_subsequent = step_ahead(motion_embeds)
    motion_successor = step_ahead(motion_subsequent)
    weights_prior = pairing_weights(
        picture_embeds,
        motion_predecessor,
        sharpness_coefficient,
        additive_shift,
        objective_coefficient,
        None,
    )
    weights_upcoming = pairing_weights(
        picture_embeds,
        motion_subsequent,
        sharpness_coefficient,
        additive_shift,
        objective_coefficient,
        None,
    )
    weights_following = pairing_weights(
        picture_embeds,
        motion_successor,
        sharpness_coefficient,
        additive_shift,
        objective_coefficient,
        None,
    )
    grad_img = grad_img + apply_rows(weights_prior, motion_predecessor)
    grad_img = grad_img + apply_rows(weights_upcoming, motion_subsequent)
    grad_img = grad_img + apply_rows(weights_following, motion_successor)
    back_terms = shifted(apply_cols(weights_prior, picture_embeds), ("gx", "gy"), -1)
    carried = apply_cols(weights_following, picture_embeds)
    carried = carry_ahead(carried) + apply_cols(weights_upcoming, picture_embeds)
    carried = carry_ahead(carried) + own_terms
    grad_sen = carried + back_terms
    return (grad_img.astype(jnp.bfloat16), grad_sen.astype(jnp.bfloat16))


def solution(mesh):
    return jax.shard_map(
        per_device,
        mesh=mesh,
        in_specs=(
            P(("gx", "gy"), None),
            P(("gx", "gy"), None),
            P(("gx", "gy"), None),
            P(),
            P(),
            P(),
        ),
        out_specs=(P(("gx", "gy"), None), P(("gx", "gy"), None)),
        check_vma=False,
    )
```

profile of v0, /device:TPU:0, one launch (start us, length us, event | category | flops | bytes accessed | tf_op | source)
XLA Modules:
  0.0 255.1 jit_solution(5260705190478897086)
XLA Ops:
  0.6 0.0 copy-start
  0.6 6.4 %collective-permute-start.1 = (bf16[1024,1152]{1,0:T(8,128)(2,1)}, bf16[1024,1152]{1,0:T(8,128)(2,1)}, u32[]{:S(2)}, u32[]{:S(2)}) collective-permute-start(bf16[1024,1152]{1,0:T(8,128)(2,1)} %param.7), channel_id=1, source_target_pairs={{0,31},{1,0},{2,1},{3,2},{4,3},{5,4},{6,5},{7,6},{8,7},{9,8},{10,9... | collective-permute-start | bytes 7077896 | tf_op jit(solution)/shard_map/ppermute | solution.py:9
  7.1 26.7 %collective-permute-done.1 = bf16[1024,1152]{1,0:T(8,128)(2,1)} collective-permute-done((bf16[1024,1152]{1,0:T(8,128)(2,1)}, bf16[1024,1152]{1,0:T(8,128)(2,1)}, u32[]{:S(2)}, u32[]{:S(2)}) %collective-permute-start.1) | collective-permute-done | bytes 2359328 | tf_op jit(solution)/shard_map/ppermute | solution.py:9
  33.7 5.6 %collective-permute-start.2 = (bf16[1024,1152]{1,0:T(8,128)(2,1)}, bf16[1024,1152]{1,0:T(8,128)(2,1)}, u32[]{:S(2)}, u32[]{:S(2)}) collective-permute-start(bf16[1024,1152]{1,0:T(8,128)(2,1)} %collective-permute-done.1), channel_id=1, source_target_pairs={{0,31},{1,0},{2,1},{3,2},{4,3},{5,4},{6,5},{7,6},{8,7},{9,8},{10,9... | collective-permute-start | bytes 7077896 | tf_op jit(solution)/shard_map/ppermute | solution.py:9
  39.4 0.0 collective-permute-start
  41.3 44.4 %collective-permute-done.2 = bf16[1024,1152]{1,0:T(8,128)(2,1)} collective-permute-done((bf16[1024,1152]{1,0:T(8,128)(2,1)}, bf16[1024,1152]{1,0:T(8,128)(2,1)}, u32[]{:S(2)}, u32[]{:S(2)}) %collective-permute-start.2) | collective-permute-done | bytes 2359328 | tf_op jit(solution)/shard_map/ppermute | solution.py:9
  85.7 0.0 copy-done
  85.7 5.3 %multiply_convert_fusion = bf16[1024,1024]{1,0:T(8,128)(2,1)S(1)} fusion(bf16[1024,1152]{1,0:T(8,128)(2,1)S(1)} %copy-done, bf16[1024,1152]{1,0:T(8,128)(2,1)} %collective-permute-done.2, f32[]{:T(128)} %bitcast.34, f32[]{:T(128)} %bitcast.30, f32[]{:T(128)S(6)} %div.15), kind=kOutput, calls=%fused_computation.3 | convolution fusion | flops 2423259136 | bytes 6815756 | tf_op jit(solution)/shard_map/dot_general | solution.py:20
  91.0 3.0 %fusion.3 = f32[1024,1152]{1,0:T(8,128)S(1)} fusion(bf16[1024,1024]{1,0:T(8,128)(2,1)S(1)} %multiply_convert_fusion, bf16[1024,1152]{1,0:T(8,128)(2,1)S(1)} %copy-done), kind=kOutput, calls=%fused_computation.11 | convolution fusion | flops 2415919104 | bytes 9175040 | tf_op jit(solution)/shard_map/dot_general | solution.py:39
  94.0 0.1 collective-permute-start.3
  94.0 0.0 collective-permute-done
  94.0 5.3 %multiply_convert_fusion.2 = bf16[1024,1024]{1,0:T(8,128)(2,1)S(1)} fusion(bf16[1024,1152]{1,0:T(8,128)(2,1)S(1)} %copy-done, bf16[1024,1152]{1,0:T(8,128)(2,1)} %collective-permute-done, f32[]{:T(128)} %bitcast.36, f32[]{:T(128)} %bitcast.32, f32[]{:T(128)S(6)} %div.15), kind=kOutput, calls=%fused_computation.5 | convolution fusion | flops 2423259136 | bytes 6815756 | tf_op jit(solution)/shard_map/dot_general | solution.py:20
  99.3 0.0 copy-start.5
  99.4 3.0 %fusion.5 = f32[1024,1152]{1,0:T(8,128)S(1)} fusion(bf16[1024,1024]{1,0:T(8,128)(2,1)S(1)} %multiply_convert_fusion.2, bf16[1024,1152]{1,0:T(8,128)(2,1)S(1)} %copy-done), kind=kOutput, calls=%fused_computation.13 | convolution fusion | flops 2415919104 | bytes 9175040 | tf_op jit(solution)/shard_map/dot_general | solution.py:39
  102.4 0.0 copy-done.5
  102.4 5.7 %collective-permute-start.5 = (f32[1024,1152]{1,0:T(8,128)S(1)}, f32[1024,1152]{1,0:T(8,128)S(1)}, u32[]{:S(2)}, u32[]{:S(2)}) collective-permute-start(f32[1024,1152]{1,0:T(8,128)S(1)} %fusion.5), channel_id=1, source_target_pairs={{0,31},{1,0},{2,1},{3,2},{4,3},{5,4},{6,5},{7,6},{8,7},{9,8},{10,9... | collective-permute-start | bytes 14155784 | tf_op jit(solution)/shard_map/ppermute | solution.py:9
  108.1 5.3 %multiply_convert_fusion.1 = bf16[1024,1024]{1,0:T(8,128)(2,1)S(1)} fusion(bf16[1024,1152]{1,0:T(8,128)(2,1)S(1)} %copy-done, bf16[1024,1152]{1,0:T(8,128)(2,1)} %collective-permute-done.1, f32[]{:T(128)} %bitcast.35, f32[]{:T(128)} %bitcast.31, f32[]{:T(128)S(6)} %div.15), kind=kOutput, calls=%fused_computation.4 | convolution fusion | flops 2423259136 | bytes 6815756 | tf_op jit(solution)/shard_map/dot_general | solution.py:20
  113.4 0.0 copy-start.3
  113.4 0.0 copy-start.1
  113.4 0.0 copy-start.2
  113.5 79.2 %collective-permute-done.3 = f32[1024,1152]{1,0:T(8,128)S(1)} collective-permute-done((f32[1024,1152]{1,0:T(8,128)S(1)}, f32[1024,1152]{1,0:T(8,128)S(1)}, u32[]{:S(2)}, u32[]{:S(2)}) %collective-permute-start.3) | collective-permute-done | bytes 4718624 | tf_op jit(solution)/shard_map/ppermute | solution.py:9
  192.7 3.1 %convolution_add_fusion = f32[1024,1152]{1,0:T(8,128)S(1)} fusion(f32[1024,1152]{1,0:T(8,128)S(1)} %collective-permute-done.3, bf16[1024,1024]{1,0:T(8,128)(2,1)S(1)} %multiply_convert_fusion.1, bf16[1024,1152]{1,0:T(8,128)(2,1)S(1)} %copy-done), kind=kOutput, calls=%fused_computation.2 | convolution fusion | flops 2417098752 | bytes 13893632 | tf_op jit(solution)/shard_map/dot_general | solution.py:39
  195.8 0.0 copy-done.3
  195.8 0.1 collective-permute-start.4
  195.9 0.0 copy-done.1
  195.9 0.0 copy-done.2
  195.9 4.0 %multiply_convert_fusion.3 = bf16[1024,1024]{1,0:T(8,128)(2,1)S(1)} fusion(bf16[1024,1152]{1,0:T(8,128)(2,1)S(1)} %copy-done, bf16[1024,1152]{1,0:T(8,128)(2,1)S(1)} %copy-done.1, s32[1024]{0:T(1024)S(1)} %bitcast.38, f32[]{:T(128)} %bitcast.33, f32[]{:T(128)} %bitcast.29, f32[]{:T(128)S(6)} %div.15), kind=kOutput, calls=%fused_computation.6 | convolution fusion | flops 2426404864 | bytes 6819852 | tf_op jit(solution)/shard_map/dot_general | solution.py:20
  199.9 4.6 %fusion = f32[1024,1152]{1,0:T(8,128)} fusion(bf16[1024,1024]{1,0:T(8,128)(2,1)S(1)} %multiply_convert_fusion.3, bf16[1024,1152]{1,0:T(8,128)(2,1)S(1)} %copy-done.1), kind=kOutput, calls=%fused_computation.8 | convolution fusion | flops 2415919104 | bytes 9175040 | tf_op jit(solution)/shard_map/dot_general | solution.py:35
  204.5 0.0 copy-start.4
  204.5 3.0 %fusion.4 = f32[1024,1152]{1,0:T(8,128)S(1)} fusion(bf16[1024,1024]{1,0:T(8,128)(2,1)S(1)} %multiply_convert_fusion.3, bf16[1024,1152]{1,0:T(8,128)(2,1)S(1)} %copy-done), kind=kOutput, calls=%fused_computation.12 | convolution fusion | flops 2415919104 | bytes 9175040 | tf_op jit(solution)/shard_map/dot_general | solution.py:39
  207.5 0.0 copy-done.4
  207.5 0.0 copy-start.6
  207.5 6.3 %fusion.2 = f32[1024,1152]{1,0:T(8,128)} fusion(bf16[1024,1024]{1,0:T(8,128)(2,1)S(1)} %copy-done.4, bf16[1024,1152]{1,0:T(8,128)(2,1)} %collective-permute-done.1), kind=kOutput, calls=%fused_computation.10 | convolution fusion | flops 2415919104 | bytes 9175040 | tf_op jit(solution)/shard_map/dot_general | solution.py:35
  213.8 0.0 copy-done.6
  213.8 6.2 %fusion.1 = f32[1024,1152]{1,0:T(8,128)} fusion(bf16[1024,1024]{1,0:T(8,128)(2,1)S(1)} %copy-done.6, bf16[1024,1152]{1,0:T(8,128)(2,1)} %collective-permute-done), kind=kOutput, calls=%fused_computation.9 | convolution fusion | flops 2415919104 | bytes 9175040 | tf_op jit(solution)/shard_map/dot_general | solution.py:35
  220.1 8.7 %add_convert_fusion.1 = bf16[1024,1152]{1,0:T(8,128)(2,1)} fusion(f32[1024,1152]{1,0:T(8,128)} %fusion.2, f32[1024,1152]{1,0:T(8,128)} %fusion, f32[1024,1152]{1,0:T(8,128)} %fusion.1, bf16[1024,1024]{1,0:T(8,128)(2,1)S(1)} %multiply_convert_fusion, bf16[1024,1152]{1,0:T(8,128)(2,1)} %collective-permute-done.2), kind=kOutput, calls=%fused_computation.1 | convolution fusion | flops 2420637696 | bytes 20971520 | tf_op jit(solution)/shard_map/dot_general | solution.py:35
  228.7 0.0 collective-permute-done.5
  228.7 24.3 %collective-permute-done.4 = f32[1024,1152]{1,0:T(8,128)S(1)} collective-permute-done((f32[1024,1152]{1,0:T(8,128)S(1)}, f32[1024,1152]{1,0:T(8,128)S(1)}, u32[]{:S(2)}, u32[]{:S(2)}) %collective-permute-start.4) | collective-permute-done | bytes 4718624 | tf_op jit(solution)/shard_map/ppermute | solution.py:9
  253.0 2.1 add_convert_fusion
Async XLA Ops:
  0.6 85.1 %copy-start = (bf16[1024,1152]{1,0:T(8,128)(2,1)S(1)}, bf16[1024,1152]{1,0:T(8,128)(2,1)}, u32[]{:S(2)}) copy-start(bf16[1024,1152]{1,0:T(8,128)(2,1)} %param.6) | copy-start | bytes 7077892
  0.6 33.1 %collective-permute-start.1 = (bf16[1024,1152]{1,0:T(8,128)(2,1)}, bf16[1024,1152]{1,0:T(8,128)(2,1)}, u32[]{:S(2)}, u32[]{:S(2)}) collective-permute-start(bf16[1024,1152]{1,0:T(8,128)(2,1)} %param.7), channel_id=1, source_target_pairs={{0,31},{1,0},{2,1},{3,2},{4,3},{5,4},{6,5},{7,6},{8,7},{9,8},{10,9... | collective-permute-start | bytes 7077896 | tf_op jit(solution)/shard_map/ppermute | solution.py:9
  33.7 51.9 %collective-permute-start.2 = (bf16[1024,1152]{1,0:T(8,128)(2,1)}, bf16[1024,1152]{1,0:T(8,128)(2,1)}, u32[]{:S(2)}, u32[]{:S(2)}) collective-permute-start(bf16[1024,1152]{1,0:T(8,128)(2,1)} %collective-permute-done.1), channel_id=1, source_target_pairs={{0,31},{1,0},{2,1},{3,2},{4,3},{5,4},{6,5},{7,6},{8,7},{9,8},{10,9... | collective-permute-start | bytes 7077896 | tf_op jit(solution)/shard_map/ppermute | solution.py:9
  39.4 54.7 %collective-permute-start = (bf16[1024,1152]{1,0:T(8,128)(2,1)}, bf16[1024,1152]{1,0:T(8,128)(2,1)}, u32[]{:S(2)}, u32[]{:S(2)}) collective-permute-start(bf16[1024,1152]{1,0:T(8,128)(2,1)} %param.7), channel_id=1, source_target_pairs={{0,1},{1,2},{2,3},{3,4},{4,5},{5,6},{6,7},{7,8},{8,9},{9,10},{10,1... | collective-permute-start | bytes 7077896 | tf_op jit(solution)/shard_map/ppermute | solution.py:9
  94.0 98.7 %collective-permute-start.3 = (f32[1024,1152]{1,0:T(8,128)S(1)}, f32[1024,1152]{1,0:T(8,128)S(1)}, u32[]{:S(2)}, u32[]{:S(2)}) collective-permute-start(f32[1024,1152]{1,0:T(8,128)S(1)} %fusion.3), channel_id=1, source_target_pairs={{0,1},{1,2},{2,3},{3,4},{4,5},{5,6},{6,7},{7,8},{8,9},{9,10},{10,1... | collective-permute-start | bytes 14155784 | tf_op jit(solution)/shard_map/ppermute | solution.py:9
  99.3 3.0 %copy-start.5 = (bf16[1024,1024]{1,0:T(8,128)(2,1)}, bf16[1024,1024]{1,0:T(8,128)(2,1)S(1)}, u32[]{:S(2)}) copy-start(bf16[1024,1024]{1,0:T(8,128)(2,1)S(1)} %multiply_convert_fusion.2) | copy-start | bytes 6291460
  102.4 126.3 %collective-permute-start.5 = (f32[1024,1152]{1,0:T(8,128)S(1)}, f32[1024,1152]{1,0:T(8,128)S(1)}, u32[]{:S(2)}, u32[]{:S(2)}) collective-permute-start(f32[1024,1152]{1,0:T(8,128)S(1)} %fusion.5), channel_id=1, source_target_pairs={{0,31},{1,0},{2,1},{3,2},{4,3},{5,4},{6,5},{7,6},{8,7},{9,8},{10,9... | collective-permute-start | bytes 14155784 | tf_op jit(solution)/shard_map/ppermute | solution.py:9
  113.4 82.4 %copy-start.3 = (bf16[1024,1024]{1,0:T(8,128)(2,1)}, bf16[1024,1024]{1,0:T(8,128)(2,1)S(1)}, u32[]{:S(2)}) copy-start(bf16[1024,1024]{1,0:T(8,128)(2,1)S(1)} %multiply_convert_fusion.1) | copy-start | bytes 6291460
  113.4 82.4 %copy-start.1 = (bf16[1024,1152]{1,0:T(8,128)(2,1)S(1)}, bf16[1024,1152]{1,0:T(8,128)(2,1)}, u32[]{:S(2)}) copy-start(bf16[1024,1152]{1,0:T(8,128)(2,1)} %param.7) | copy-start | bytes 7077892
  113.4 82.4 %copy-start.2 = (s32[1,1024]{1,0:T(1,128)S(1)}, s32[1,1024]{1,0:T(1,128)}, u32[]{:S(2)}) copy-start(s32[1,1024]{1,0:T(1,128)} %param.8) | copy-start | bytes 12292
  195.8 57.2 %collective-permute-start.4 = (f32[1024,1152]{1,0:T(8,128)S(1)}, f32[1024,1152]{1,0:T(8,128)S(1)}, u32[]{:S(2)}, u32[]{:S(2)}) collective-permute-start(f32[1024,1152]{1,0:T(8,128)S(1)} %convolution_add_fusion), channel_id=1, source_target_pairs={{0,1},{1,2},{2,3},{3,4},{4,5},{5,6},{6,7},{7,8},{8,9},{9,10},{10,1... | collective-permute-start | bytes 14155784 | tf_op jit(solution)/shard_map/ppermute | solution.py:9
  204.5 3.0 %copy-start.4 = (bf16[1024,1024]{1,0:T(8,128)(2,1)S(1)}, bf16[1024,1024]{1,0:T(8,128)(2,1)}, u32[]{:S(2)}) copy-start(bf16[1024,1024]{1,0:T(8,128)(2,1)} %copy-done.3) | copy-start | bytes 6291460
  207.5 6.3 %copy-start.6 = (bf16[1024,1024]{1,0:T(8,128)(2,1)S(1)}, bf16[1024,1024]{1,0:T(8,128)(2,1)}, u32[]{:S(2)}) copy-start(bf16[1024,1024]{1,0:T(8,128)(2,1)} %copy-done.5) | copy-start | bytes 6291460
where the time goes:
time: 255 us
  waiting for transfers between devices  175 us (69%)
  matrix products  57.7 us (23%)
  starting transfers between devices  17.9 us (7%)
  between operations  2.76 us (1%)
    ppermute x6, waiting for transfers between devices, shifted(): lax.ppermute(value, axis, [(i, (i + by) % devices) for i in range(devices)])  175 us
    dot_general x4, matrix products, apply_rows(): return jnp.dot(weights, eastern_entries, preferred_element_type=jnp.float32)  25.8 us
    dot_general x4, matrix products, pairing_weights(): lax.dot_general(western_entries, eastern_entries, (((1,), (1,)), ((), ())...  19.8 us
    ppermute x6, starting transfers between devices, shifted(): lax.ppermute(value, axis, [(i, (i + by) % devices) for i in range(devices)])  17.9 us
    dot_general x4, matrix products, apply_cols(): lax.dot_general(weights, western_entries, (((0,), (0,)), ((), ())), prefe...  12.1 us
  transfers between devices with their start and end apart: 6, of which 4 were waited for; matrix products, arithmetic and copies ran while one was open for 23% of the time, Pallas kernels for 0%

commit v1 on v0

v1 whole, which is shorter than its diff:
```python
import jax
import jax.numpy as jnp
from jax import lax
from jax.sharding import PartitionSpec as P

AXES = ("gx", "gy")


def shifted(value, by):
    n = lax.axis_size(AXES)
    return lax.ppermute(value, AXES, [(i, (i + by) % n) for i in range(n)])


def swapped(value):
    n = lax.axis_size(AXES)
    return lax.ppermute(value, AXES, [(i, i ^ 1) for i in range(n)])


def pair_weights(own, other, sharpness, shift, objective, target):
    logits = lax.dot_general(
        own, other, (((1,), (1,)), ((), ())), preferred_element_type=jnp.float32
    )
    slope = jax.nn.sigmoid(sharpness[0] * logits + shift[0])
    if target is not None:
        slope = slope - target
    return (objective * slope).astype(jnp.bfloat16)


def per_device(image, sensor, match, sharpness, shift, gain):
    rows = image.shape[0]
    n = lax.axis_size(AXES)
    objective = gain[0] * sharpness[0] / (rows * n)
    first_core = lax.rem(lax.axis_index(AXES), 2) == 0
    sensor_two = shifted(sensor, -2)
    image_two = shifted(image, 2)
    sensor_before = shifted(sensor, 1)
    image_after = shifted(image, -1)
    sensor_after = swapped(jnp.where(first_core, sensor_two, sensor))
    image_before = swapped(jnp.where(first_core, image, image_two))
    columns = jnp.arange(rows, dtype=jnp.int32)
    target = (match[0][:, None] == columns[None, :]).astype(jnp.float32)
    weights = pair_weights(image, sensor, sharpness, shift, objective, target)

    def dot(a, b):
        return jnp.dot(a, b, preferred_element_type=jnp.float32)

    grad_image = dot(weights, sensor)
    grad_sensor = lax.dot_general(
        weights, image, (((0,), (0,)), ((), ())), preferred_element_type=jnp.float32
    )
    for other in (sensor_before, sensor_after, sensor_two):
        grad_image += dot(pair_weights(image, other, sharpness, shift, objective, None), other)
    for other in (image_after, image_before, image_two):
        grad_sensor += dot(pair_weights(sensor, other, sharpness, shift, objective, None), other)
    return grad_image.astype(jnp.bfloat16), grad_sensor.astype(jnp.bfloat16)


def solution(mesh):
    rows = P(AXES, None)
    return jax.shard_map(
        per_device,
        mesh=mesh,
        in_specs=(rows, rows, rows, P(), P(), P()),
        out_specs=(rows, rows),
        check_vma=False,
    )
```

time: 255 us -> 235 us (0.922)
  waiting for transfers between devices: 175 us -> 129 us
  matrix products: 57.7 us -> 90.2 us
  starting transfers between devices: 17.9 us -> 8.29 us
  other arithmetic: 2.07 us -> 5 us
    ppermute x6, waiting for transfers between devices: 175 us -> 129 us  [the longest x4 129 us: shifted(): return lax.ppermute(value, AXES, [(i, (i + by) % n) for i in range(n)])]
    dot_general x12 -> x9, matrix products: 57.7 us -> 90.2 us  [the longest x7 79.3 us: dot(): return jnp.dot(a, b, preferred_element_type=jnp.float32)]
    ppermute x6, starting transfers between devices: 17.9 us -> 8.29 us  [the longest x4 8.17 us: shifted(): return lax.ppermute(value, AXES, [(i, (i + by) % n) for i in range(n)])]
    select_n x0 -> x2, other arithmetic: none -> 5 us  [the longest x1 3.33 us: per_device(): sensor_after = swapped(jnp.where(first_core, sensor_two, sensor))]
  transfers between devices with their start and end apart: 6 -> 6, of which waited for: 4 -> 2; matrix products, arithmetic and copies ran while one was open for 23% -> 24% of each run, Pallas kernels for 0% -> 0%
where the time goes in v1:
time: 235 us
  waiting for transfers between devices  129 us (55%)
  matrix products  90.2 us (38%)
  starting transfers between devices  8.29 us (4%)
  other arithmetic  5 us (2%)
  between operations  2.63 us (1%)
    ppermute x4, waiting for transfers between devices, shifted(): return lax.ppermute(value, AXES, [(i, (i + by) % n) for i in range(n)])  129 us
    dot_general x7, matrix products, dot(): return jnp.dot(a, b, preferred_element_type=jnp.float32)  79.3 us
    ppermute x4, starting transfers between devices, shifted(): return lax.ppermute(value, AXES, [(i, (i + by) % n) for i in range(n)])  8.17 us
    dot_general x1, matrix products, pair_weights(): lax.dot_general(own, other, (((1,), (1,)), ((), ())), preferred_element_t...  6.26 us
  transfers between devices with their start and end apart: 6, of which 2 were waited for; matrix products, arithmetic and copies ran while one was open for 24% of the time, Pallas kernels for 0%

profile of v1, /device:TPU:0, one launch (start us, length us, event | category | flops | bytes accessed | tf_op | source)
XLA Modules:
  0.0 234.7 jit_solution(6407184865801526419)
XLA Ops:
  0.6 3.1 %collective-permute-start.4 = (bf16[1024,1152]{1,0:T(8,128)(2,1)}, bf16[1024,1152]{1,0:T(8,128)(2,1)}, u32[]{:S(2)}, u32[]{:S(2)}) collective-permute-start(bf16[1024,1152]{1,0:T(8,128)(2,1)} %param.6), channel_id=1, source_target_pairs={{0,2},{1,3},{2,4},{3,5},{4,6},{5,7},{6,8},{7,9},{8,10},{9,11},{10,... | collective-permute-start | bytes 7077896 | tf_op jit(solution)/shard_map/ppermute | solution.py:11
  3.7 3.4 %collective-permute-start.3 = (bf16[1024,1152]{1,0:T(8,128)(2,1)}, bf16[1024,1152]{1,0:T(8,128)(2,1)}, u32[]{:S(2)}, u32[]{:S(2)}) collective-permute-start(bf16[1024,1152]{1,0:T(8,128)(2,1)} %param.6), channel_id=1, source_target_pairs={{0,31},{1,0},{2,1},{3,2},{4,3},{5,4},{6,5},{7,6},{8,7},{9,8},{10,9... | collective-permute-start | bytes 7077896 | tf_op jit(solution)/shard_map/ppermute | solution.py:11
  7.1 1.7 collective-permute-start.1
  8.8 0.0 collective-permute-start
  10.8 0.0 copy-start.1
  10.8 6.3 %multiply_convert_fusion.6 = bf16[1024,1024]{1,0:T(8,128)(2,1)S(1)} fusion(bf16[1024,1152]{1,0:T(8,128)(2,1)} %param.6, bf16[1024,1152]{1,0:T(8,128)(2,1)} %param.7, s32[1024]{0:T(1024)} %bitcast.44, f32[]{:T(128)} %bitcast.36, f32[]{:T(128)} %bitcast.29, f32[]{:T(128)S(6)} %div.24), kind=kOutput, calls=%fused_computation.8 | convolution fusion | flops 2426404864 | bytes 6819852 | tf_op jit(solution)/shard_map/dot_general | solution.py:20
  17.0 0.0 copy-done.1
  17.0 0.0 copy-start.3
  17.1 0.0 copy-start
  17.1 4.7 %fusion.13 = f32[1024,1152]{1,0:T(8,128)} fusion(bf16[1024,1024]{1,0:T(8,128)(2,1)S(1)} %multiply_convert_fusion.6, bf16[1024,1152]{1,0:T(8,128)(2,1)S(1)} %copy-done.1), kind=kOutput, calls=%fused_computation.25 | convolution fusion | flops 2415919104 | bytes 9175040 | tf_op jit(solution)/shard_map/dot_general | solution.py:48
  21.7 0.0 copy-done.3
  21.7 0.0 copy-done
  21.7 0.0 copy-start.2
  21.7 6.7 %fusion.12 = f32[1024,1152]{1,0:T(8,128)} fusion(bf16[1024,1024]{1,0:T(8,128)(2,1)} %copy-done.3, bf16[1024,1152]{1,0:T(8,128)(2,1)S(1)} %copy-done), kind=kOutput, calls=%fused_computation.24 | convolution fusion | flops 2415919104 | bytes 9175040 | tf_op jit(solution)/shard_map/dot_general | solution.py:45
  28.5 31.6 %collective-permute-done.4 = bf16[1024,1152]{1,0:T(8,128)(2,1)} collective-permute-done((bf16[1024,1152]{1,0:T(8,128)(2,1)}, bf16[1024,1152]{1,0:T(8,128)(2,1)}, u32[]{:S(2)}, u32[]{:S(2)}) %collective-permute-start.4) | collective-permute-done | bytes 2359328 | tf_op jit(solution)/shard_map/ppermute | solution.py:11
  60.1 0.0 copy-done.2
  60.1 1.7 broadcast_select_fusion
  61.7 0.1 collective-permute-start.5
  61.8 97.0 %collective-permute-done.1 = bf16[1024,1152]{1,0:T(8,128)(2,1)} collective-permute-done((bf16[1024,1152]{1,0:T(8,128)(2,1)}, bf16[1024,1152]{1,0:T(8,128)(2,1)}, u32[]{:S(2)}, u32[]{:S(2)}) %collective-permute-start.1) | collective-permute-done | bytes 2359328 | tf_op jit(solution)/shard_map/ppermute | solution.py:11
  158.8 3.3 %broadcast_select_fusion.1 = bf16[1024,1152]{1,0:T(8,128)(2,1)} fusion(bf16[1024,1152]{1,0:T(8,128)(2,1)} %collective-permute-done.1, bf16[1024,1152]{1,0:T(8,128)(2,1)S(1)} %copy-done, pred[]{:T(512)S(6)} %eq.22), kind=kLoop, calls=%fused_computation.11 | loop fusion | flops 1179648 | bytes 7077889 | tf_op jit(solution)/shard_map/jit(_where)/select_n | solution.py:38
  162.1 0.0 collective-permute-start.2
  162.1 0.0 collective-permute-done.3
  162.1 10.3 %fusion.2 = f32[1024,1152]{1,0:T(8,128)} fusion(bf16[1024,1152]{1,0:T(8,128)(2,1)} %collective-permute-done.3, bf16[1024,1152]{1,0:T(8,128)(2,1)S(1)} %copy-done, f32[]{:T(128)} %bitcast.39, f32[]{:T(128)} %bitcast.32, f32[]{:T(128)S(6)} %div.24), kind=kOutput, calls=%fused_computation.14 | convolution fusion | flops 4839178240 | bytes 9437196 | tf_op jit(solution)/shard_map/dot_general | solution.py:45
  172.5 0.0 collective-permute-done
  172.5 11.0 %fusion = f32[1024,1152]{1,0:T(8,128)} fusion(bf16[1024,1152]{1,0:T(8,128)(2,1)} %collective-permute-done, bf16[1024,1152]{1,0:T(8,128)(2,1)} %param.6, f32[]{:T(128)} %bitcast.42, f32[]{:T(128)} %bitcast.35, f32[]{:T(128)S(6)} %div.24), kind=kOutput, calls=%fused_computation.12 | convolution fusion | flops 4839178240 | bytes 9437196 | tf_op jit(solution)/shard_map/dot_general | solution.py:45
  183.5 0.0 collective-permute-done.5
  183.5 11.3 %fusion.5 = f32[1024,1152]{1,0:T(8,128)} fusion(bf16[1024,1152]{1,0:T(8,128)(2,1)} %collective-permute-done.5, bf16[1024,1152]{1,0:T(8,128)(2,1)S(1)} %copy-done, f32[]{:T(128)} %bitcast.38, f32[]{:T(128)} %bitcast.31, f32[]{:T(128)S(6)} %div.24), kind=kOutput, calls=%fused_computation.17 | convolution fusion | flops 4839178240 | bytes 9437196 | tf_op jit(solution)/shard_map/dot_general | solution.py:45
  194.8 0.0 collective-permute-done.2
  194.8 11.7 %fusion.4 = f32[1024,1152]{1,0:T(8,128)} fusion(bf16[1024,1152]{1,0:T(8,128)(2,1)} %collective-permute-done.2, bf16[1024,1152]{1,0:T(8,128)(2,1)} %param.6, f32[]{:T(128)} %bitcast.41, f32[]{:T(128)} %bitcast.34, f32[]{:T(128)S(6)} %div.24), kind=kOutput, calls=%fused_computation.16 | convolution fusion | flops 4839178240 | bytes 9437196 | tf_op jit(solution)/shard_map/dot_general | solution.py:45
  206.5 13.5 %add_convert_fusion = bf16[1024,1152]{1,0:T(8,128)(2,1)} fusion(f32[1024,1152]{1,0:T(8,128)} %fusion.5, f32[1024,1152]{1,0:T(8,128)} %fusion.13, f32[1024,1152]{1,0:T(8,128)} %fusion.2, bf16[1024,1152]{1,0:T(8,128)(2,1)} %collective-permute-done.4, bf16[1024,1152]{1,0:T(8,128)(2,1)S(1)} %copy-done, f32[]{:T(128)} %bitcast.37, f32[]{:T(128)} %bitcast.30, ...), kind=kOutput, calls=%fused_computation | convolution fusion | flops 4843896832 | bytes 21233676 | tf_op jit(solution)/shard_map/dot_general | solution.py:45
  220.0 14.7 %add_convert_fusion.1 = bf16[1024,1152]{1,0:T(8,128)(2,1)} fusion(f32[1024,1152]{1,0:T(8,128)} %fusion.4, f32[1024,1152]{1,0:T(8,128)} %fusion.12, f32[1024,1152]{1,0:T(8,128)} %fusion, bf16[1024,1152]{1,0:T(8,128)(2,1)} %collective-permute-done.1, bf16[1024,1152]{1,0:T(8,128)(2,1)} %param.6, f32[]{:T(128)} %bitcast.40, f32[]{:T(128)} %bitcast.33, f32[]{:T(128)S(6)} %div.24), kind=kOutput, calls=%fused_computation.1 | convolution fusion | flops 4843896832 | bytes 21233676 | tf_op jit(solution)/shard_map/dot_general | solution.py:45
Async XLA Ops:
  0.6 59.4 %collective-permute-start.4 = (bf16[1024,1152]{1,0:T(8,128)(2,1)}, bf16[1024,1152]{1,0:T(8,128)(2,1)}, u32[]{:S(2)}, u32[]{:S(2)}) collective-permute-start(bf16[1024,1152]{1,0:T(8,128)(2,1)} %param.6), channel_id=1, source_target_pairs={{0,2},{1,3},{2,4},{3,5},{4,6},{5,7},{6,8},{7,9},{8,10},{9,11},{10,... | collective-permute-start | bytes 7077896 | tf_op jit(solution)/shard_map/ppermute | solution.py:11
  3.7 158.4 %collective-permute-start.3 = (bf16[1024,1152]{1,0:T(8,128)(2,1)}, bf16[1024,1152]{1,0:T(8,128)(2,1)}, u32[]{:S(2)}, u32[]{:S(2)}) collective-permute-start(bf16[1024,1152]{1,0:T(8,128)(2,1)} %param.6), channel_id=1, source_target_pairs={{0,31},{1,0},{2,1},{3,2},{4,3},{5,4},{6,5},{7,6},{8,7},{9,8},{10,9... | collective-permute-start | bytes 7077896 | tf_op jit(solution)/shard_map/ppermute | solution.py:11
  7.1 151.7 %collective-permute-start.1 = (bf16[1024,1152]{1,0:T(8,128)(2,1)}, bf16[1024,1152]{1,0:T(8,128)(2,1)}, u32[]{:S(2)}, u32[]{:S(2)}) collective-permute-start(bf16[1024,1152]{1,0:T(8,128)(2,1)} %param.7), channel_id=1, source_target_pairs={{0,30},{1,31},{2,0},{3,1},{4,2},{5,3},{6,4},{7,5},{8,6},{9,7},{10,... | collective-permute-start | bytes 7077896 | tf_op jit(solution)/shard_map/ppermute | solution.py:11
  8.8 163.7 %collective-permute-start = (bf16[1024,1152]{1,0:T(8,128)(2,1)}, bf16[1024,1152]{1,0:T(8,128)(2,1)}, u32[]{:S(2)}, u32[]{:S(2)}) collective-permute-start(bf16[1024,1152]{1,0:T(8,128)(2,1)} %param.7), channel_id=1, source_target_pairs={{0,1},{1,2},{2,3},{3,4},{4,5},{5,6},{6,7},{7,8},{8,9},{9,10},{10,1... | collective-permute-start | bytes 7077896 | tf_op jit(solution)/shard_map/ppermute | solution.py:11
  10.8 6.3 %copy-start.1 = (bf16[1024,1152]{1,0:T(8,128)(2,1)S(1)}, bf16[1024,1152]{1,0:T(8,128)(2,1)}, u32[]{:S(2)}) copy-start(bf16[1024,1152]{1,0:T(8,128)(2,1)} %param.6) | copy-start | bytes 7077892
  17.0 4.7 %copy-start.3 = (bf16[1024,1024]{1,0:T(8,128)(2,1)}, bf16[1024,1024]{1,0:T(8,128)(2,1)S(1)}, u32[]{:S(2)}) copy-start(bf16[1024,1024]{1,0:T(8,128)(2,1)S(1)} %multiply_convert_fusion.6) | copy-start | bytes 6291460
  17.1 4.7 %copy-start = (bf16[1024,1152]{1,0:T(8,128)(2,1)S(1)}, bf16[1024,1152]{1,0:T(8,128)(2,1)}, u32[]{:S(2)}) copy-start(bf16[1024,1152]{1,0:T(8,128)(2,1)} %param.7) | copy-start | bytes 7077892
  21.7 38.3 %copy-start.2 = (bf16[1024,1152]{1,0:T(8,128)(2,1)S(1)}, bf16[1024,1152]{1,0:T(8,128)(2,1)}, u32[]{:S(2)}) copy-start(bf16[1024,1152]{1,0:T(8,128)(2,1)} %param.6) | copy-start | bytes 7077892
  61.7 121.8 %collective-permute-start.5 = (bf16[1024,1152]{1,0:T(8,128)(2,1)}, bf16[1024,1152]{1,0:T(8,128)(2,1)}, u32[]{:S(2)}, u32[]{:S(2)}) collective-permute-start(bf16[1024,1152]{1,0:T(8,128)(2,1)} %broadcast_select_fusion), channel_id=1, source_target_pairs={{0,1},{1,0},{2,3},{3,2},{4,5},{5,4},{6,7},{7,6},{8,9},{9,8},{10,11... | collective-permute-start | bytes 7077896 | tf_op jit(solution)/shard_map/ppermute | solution.py:16
  162.1 32.7 %collective-permute-start.2 = (bf16[1024,1152]{1,0:T(8,128)(2,1)}, bf16[1024,1152]{1,0:T(8,128)(2,1)}, u32[]{:S(2)}, u32[]{:S(2)}) collective-permute-start(bf16[1024,1152]{1,0:T(8,128)(2,1)} %broadcast_select_fusion.1), channel_id=1, source_target_pairs={{0,1},{1,0},{2,3},{3,2},{4,5},{5,4},{6,7},{7,6},{8,9},{9,8},{10,11... | collective-permute-start | bytes 7077896 | tf_op jit(solution)/shard_map/ppermute | solution.py:16

commit v2 on v1

v2 whole, which is shorter than its diff:
```python
import functools

import jax
import jax.numpy as jnp
from jax import lax
from jax.experimental import pallas as pl
from jax.experimental.pallas import tpu as pltpu
from jax.sharding import PartitionSpec as P

AXES = ("gx", "gy")
MESH = pl.DeviceIdType.MESH
SIB_SENSOR, SIB_IMAGE, TWO_SENSOR, TWO_IMAGE, FORWARDED, FAR = range(6)
CHUNK = 256
TILE = 512


def kernel(
    sizes,
    image_hbm,
    sensor_hbm,
    match_ref,
    sharpness_ref,
    shift_ref,
    gain_ref,
    grad_image_hbm,
    grad_sensor_hbm,
    own,
    got,
    acc,
    stage,
    load_sem,
    store_sem,
    send_sem,
    recv_sem,
):
    per_row, total_devices = sizes[1], sizes[0] * sizes[1]
    rows = own.shape[1]
    chunks, tiles = rows // CHUNK, rows // TILE
    me = lax.axis_index("gx") * per_row + lax.axis_index("gy")
    core = lax.rem(me, 2)

    def place(index):
        index = lax.rem(index + total_devices, total_devices)
        return (lax.div(index, per_row), lax.rem(index, per_row))

    sibling = place(me + 1 - 2 * core)
    above, below = place(me + 2), place(me - 2)
    beside = place(me - 1 + 2 * core)

    loads = [
        pltpu.make_async_copy(image_hbm, own.at[0], load_sem.at[0]),
        pltpu.make_async_copy(sensor_hbm, own.at[1], load_sem.at[1]),
    ]
    for load in loads:
        load.start()
    barrier = pltpu.get_barrier_semaphore()
    for device in (sibling, above, below, beside):
        pl.semaphore_signal(barrier, inc=1, device_id=device, device_id_type=MESH)
    pl.semaphore_wait(barrier, 4)
    for load in loads:
        load.wait()

    def part(c):
        return pl.ds(pl.multiple_of(c * CHUNK, CHUNK), CHUNK)

    def copy(role, c):
        source, device = {
            SIB_SENSOR: (lambda: own.at[1, part(c)], sibling),
            SIB_IMAGE: (lambda: own.at[0, part(c)], sibling),
            TWO_SENSOR: (lambda: own.at[1, part(c)], below),
            TWO_IMAGE: (lambda: own.at[0, part(c)], above),
            FORWARDED: (lambda: got.at[TWO_SENSOR + core, part(c)], sibling),
            FAR: (lambda: own.at[core, part(c)], beside),
        }[role]
        return pltpu.make_async_remote_copy(
            src_ref=source(),
            dst_ref=got.at[role, part(c)],
            send_sem=send_sem.at[role, c],
            recv_sem=recv_sem.at[role, c],
            device_id=device,
            device_id_type=MESH,
        )

    def each(count, body):
        lax.fori_loop(0, count, lambda i, _: (body(i), 0)[1], 0)

    def send_far(c):
        for role in (TWO_SENSOR, TWO_IMAGE, FAR):
            copy(role, c).start()

    def send_near(c):
        for role in (SIB_SENSOR, SIB_IMAGE):
            copy(role, c).start()

    each(chunks, send_far)
    each(chunks, send_near)

    sharpness, shift = sharpness_ref[0], shift_ref[0]
    objective = gain_ref[0] * sharpness / (rows * total_devices)

    def slope(mine, other):
        logits = lax.dot_general(
            mine, other, (((1,), (1,)), ((), ())), preferred_element_type=jnp.float32
        )
        return jax.nn.sigmoid(sharpness * logits + shift)

    def own_pair(c):
        other = own[0, part(c)]
        matched = match_ref[:, part(c)]

        def tile(t):
            span = pl.ds(pl.multiple_of(t * TILE, TILE), TILE)
            mine = own[1, span]
            column = t * TILE + lax.broadcasted_iota(jnp.int32, (TILE, CHUNK), 0)
            positive = (column == matched).astype(jnp.float32)
            weights = (objective * (slope(mine, other) - positive)).astype(jnp.bfloat16)
            term = jnp.dot(weights, other, preferred_element_type=jnp.float32)
            back = lax.dot_general(
                weights, mine, (((0,), (0,)), ((), ())), preferred_element_type=jnp.float32
            )

            acc[1, span] += term
            acc[0, part(c)] += back

        each(tiles, tile)

    acc[...] = jnp.zeros_like(acc)
    each(chunks, own_pair)

    def add_pair(side, role, c):
        other_at = part(c)

        def tile(t):
            span = pl.ds(pl.multiple_of(t * TILE, TILE), TILE)
            other = got[role, other_at]
            weights = (objective * slope(own[side, span], other)).astype(jnp.bfloat16)
            acc[side, span] += jnp.dot(weights, other, preferred_element_type=jnp.float32)

        each(tiles, tile)

    def near(c):
        for side, role in ((0, SIB_SENSOR), (1, SIB_IMAGE)):
            copy(role, c).wait_recv()
            add_pair(side, role, c)

    each(chunks, near)

    def remote(c):
        for role in (TWO_SENSOR, TWO_IMAGE):
            copy(role, c).wait_recv()
        copy(FORWARDED, c).start()
        add_pair(0, TWO_SENSOR, c)
        add_pair(1, TWO_IMAGE, c)
        copy(FAR, c).wait_recv()
        add_pair(core, FAR, c)
        copy(FORWARDED, c).wait_recv()
        add_pair(1 - core, FORWARDED, c)

    each(chunks, remote)

    outs = (grad_image_hbm, grad_sensor_hbm)

    def store(side, t):
        span = pl.ds(pl.multiple_of(t * TILE, TILE), TILE)
        return pltpu.make_async_copy(
            stage.at[side, span], outs[side].at[span], store_sem.at[side, t]
        )

    def finish(t):
        span = pl.ds(pl.multiple_of(t * TILE, TILE), TILE)
        for side in range(2):
            stage[side, span] = acc[side, span].astype(jnp.bfloat16)
            store(side, t).start()

    each(tiles, finish)

    def sent(c):
        for role in range(6):
            copy(role, c).wait_send()

    each(chunks, sent)
    for side in range(2):
        each(tiles, functools.partial(lambda side, t: store(side, t).wait(), side))


def per_device(sizes, image, sensor, match, sharpness, shift, gain):
    rows, width = image.shape
    anywhere = pl.BlockSpec(memory_space=pl.ANY)
    scalar = pl.BlockSpec(memory_space=pltpu.SMEM)
    chunks, tiles = rows // CHUNK, rows // TILE
    return pl.pallas_call(
        functools.partial(kernel, sizes),
        out_shape=[jax.ShapeDtypeStruct((rows, width), jnp.bfloat16)] * 2,
        in_specs=[anywhere, anywhere, pl.BlockSpec(memory_space=pltpu.VMEM)] + [scalar] * 3,
        out_specs=[anywhere, anywhere],
        scratch_shapes=[
            pltpu.VMEM((2, rows, width), jnp.bfloat16),
            pltpu.VMEM((6, rows, width), jnp.bfloat16),
            pltpu.VMEM((2, rows, width), jnp.float32),
            pltpu.VMEM((2, rows, width), jnp.bfloat16),
            pltpu.SemaphoreType.DMA((2,)),
            pltpu.SemaphoreType.DMA((2, tiles)),
            pltpu.SemaphoreType.DMA((6, chunks)),
            pltpu.SemaphoreType.DMA((6, chunks)),
        ],
        compiler_params=pltpu.CompilerParams(
            collective_id=0, has_side_effects=True, vmem_limit_bytes=56 * 2**20
        ),
        cost_estimate=pl.CostEstimate(
            flops=32 * rows * rows * width,
            bytes_accessed=8 * rows * width,
            transcendentals=8 * rows * rows,
        ),
    )(image, sensor, match, sharpness, shift, gain)


def solution(mesh):
    rows = P(AXES, None)
    sizes = tuple(mesh.shape[axis] for axis in AXES)
    return jax.shard_map(
        functools.partial(per_device, sizes),
        mesh=mesh,
        in_specs=(rows, rows, rows, P(), P(), P()),
        out_specs=(rows, rows),
        check_vma=False,
    )
```

time: 235 us -> 178 us (0.76)
  Pallas kernels: 0 us -> 171 us
  waiting for transfers between devices: 129 us -> 0 us
  matrix products: 90.2 us -> 0 us
  starting transfers between devices: 8.29 us -> 0 us
  other arithmetic: 5 us -> 0 us
  local copies, waits for them, and re-layouts: 0.02 us -> 4.81 us
    pallas_call x0 -> x1, Pallas kernels: none -> 171 us  [per_device(): pl.pallas_call(functools.partial(kernel, sizes), out_shape=[jax.ShapeDtyp...]
    ppermute x6 -> x0, waiting for transfers between devices: 129 us -> none  [the longest x4 129 us: shifted(): return lax.ppermute(value, AXES, [(i, (i + by) % n) for i in range(n)])]
    dot_general x9 -> x0, matrix products: 90.2 us -> none  [the longest x7 79.3 us: dot(): return jnp.dot(a, b, preferred_element_type=jnp.float32)]
    ppermute x6 -> x0, starting transfers between devices: 8.29 us -> none  [the longest x4 8.17 us: shifted(): return lax.ppermute(value, AXES, [(i, (i + by) % n) for i in range(n)])]
    select_n x2 -> x0, other arithmetic: 5 us -> none  [the longest x1 3.33 us: per_device(): sensor_after = swapped(jnp.where(first_core, sensor_two, sensor))]
    unnamed x8 -> x4, local copies, waits for them, and re-layouts: 0.02 us -> 4.81 us
  transfers between devices with their start and end apart: 6 -> 0, of which waited for: 2 -> 0; matrix products, arithmetic and copies ran while one was open for 24% -> 0% of each run, Pallas kernels for 0% -> 0%
where the time goes in v2:
time: 178 us
  Pallas kernels  171 us (96%)
  local copies, waits for them, and re-layouts  4.81 us (3%)
  between operations  2.58 us (1%)
    pallas_call x1, Pallas kernels, per_device(): pl.pallas_call(functools.partial(kernel, sizes), out_shape=[jax.ShapeDtyp...  171 us
    unnamed x4, local copies, waits for them, and re-layouts  4.81 us

profile of v2, /device:TPU:0, one launch (start us, length us, event | category | flops | bytes accessed | tf_op | source)
XLA Modules:
  0.0 178.0 jit_solution(11055139806587915649)
XLA Ops:
  2.6 170.6 %shard_map.77 = (bf16[1024,1152]{1,0:T(8,128)(2,1)}, bf16[1024,1152]{1,0:T(8,128)(2,1)}) custom-call(bf16[1024,1152]{1,0:T(8,128)(2,1)} %image_hbm.1, bf16[1024,1152]{1,0:T(8,128)(2,1)} %sensor_hbm.1, s32[1,1024]{1,0:T(1,128)} %match_ref.1, f32[1]{0:T(128)S(6)} %copy.10.sharpness_ref, f32[1]{0:T(128)S(6)} %copy.11.shift_ref, f32[1]{0:T(128)S(6)} %copy.12.gain_ref), custom_call_target="tpu_custom_call" | custom-call | flops 38654705664 | bytes 9437184 | tf_op jit(solution)/shard_map/pallas_call | solution.py:191
  173.2 0.0 copy-start
  173.2 3.4 %copy.13 = bf16[1024,1152]{1,0:T(8,128)(2,1)} copy(bf16[1024,1152]{1,0:T(8,128)(2,1)} %get-tuple-element.4) | data formatting | bytes 4718592
  176.6 0.0 copy-done
  176.6 1.4 copy.14
Async XLA Ops:
  173.2 3.4 %copy-start = (bf16[1024,1152]{1,0:T(8,128)(2,1)S(1)}, bf16[1024,1152]{1,0:T(8,128)(2,1)}, u32[]{:S(2)}) copy-start(bf16[1024,1152]{1,0:T(8,128)(2,1)} %get-tuple-element.5) | copy-start | bytes 7077892

commit v3 on v2

--- a/solution.py
+++ b/solution.py
@@ -22,14 +22,12 @@
     sharpness_ref,
     shift_ref,
     gain_ref,
-    grad_image_hbm,
-    grad_sensor_hbm,
+    grad_image_ref,
+    grad_sensor_ref,
     own,
     got,
     acc,
-    stage,
     load_sem,
-    store_sem,
     send_sem,
     recv_sem,
 ):
@@ -85,7 +83,7 @@
         lax.fori_loop(0, count, lambda i, _: (body(i), 0)[1], 0)
 
     def send_far(c):
-        for role in (TWO_SENSOR, TWO_IMAGE, FAR):
+        for role in (TWO_SENSOR, TWO_IMAGE):
             copy(role, c).start()
 
     def send_near(c):
@@ -93,6 +91,7 @@
             copy(role, c).start()
 
     each(chunks, send_far)
+    each(chunks, lambda c: copy(FAR, c).start())
     each(chunks, send_near)
 
     sharpness, shift = sharpness_ref[0], shift_ref[0]
@@ -103,6 +102,9 @@
             mine, other, (((1,), (1,)), ((), ())), preferred_element_type=jnp.float32
         )
         return jax.nn.sigmoid(sharpness * logits + shift)
+
+    def tile_rows(t):
+        return pl.ds(pl.multiple_of(t * TILE, TILE), TILE)
 
     def own_pair(c):
         other = own[0, part(c)]
@@ -127,14 +129,22 @@
     acc[...] = jnp.zeros_like(acc)
     each(chunks, own_pair)
 
-    def add_pair(side, role, c):
-        other_at = part(c)
-
+    def add_pair(side, role, c, last=False):
         def tile(t):
-            span = pl.ds(pl.multiple_of(t * TILE, TILE), TILE)
-            other = got[role, other_at]
+            span = tile_rows(t)
+            other = got[role, part(c)]
             weights = (objective * slope(own[side, span], other)).astype(jnp.bfloat16)
-            acc[side, span] += jnp.dot(weights, other, preferred_element_type=jnp.float32)
+            term = jnp.dot(weights, other, preferred_element_type=jnp.float32)
+            if last:
+                total = (acc[side, span] + term).astype(jnp.bfloat16)
+                for out_side, out in enumerate((grad_image_ref, grad_sensor_ref)):
+
+                    @pl.when(side == out_side)
+                    def _(out=out):
+                        out[span] = total
+
+            else:
+                acc[side, span] += term
 
         each(tiles, tile)
 
@@ -144,6 +154,10 @@
             add_pair(side, role, c)
 
     each(chunks, near)
+
+    def shared(c, last=False):
+        copy(FORWARDED, c).wait_recv()
+        add_pair(1 - core, FORWARDED, c, last)
 
     def remote(c):
         for role in (TWO_SENSOR, TWO_IMAGE):
@@ -151,60 +165,48 @@
         copy(FORWARDED, c).start()
         add_pair(0, TWO_SENSOR, c)
         add_pair(1, TWO_IMAGE, c)
+
+        @pl.when(c > 0)
+        def _():
+            shared(c - 1)
+
+    each(chunks, remote)
+    shared(chunks - 1, True)
+
+    def far(c, last=False):
         copy(FAR, c).wait_recv()
-        add_pair(core, FAR, c)
-        copy(FORWARDED, c).wait_recv()
-        add_pair(1 - core, FORWARDED, c)
-
-    each(chunks, remote)
-
-    outs = (grad_image_hbm, grad_sensor_hbm)
-
-    def store(side, t):
-        span = pl.ds(pl.multiple_of(t * TILE, TILE), TILE)
-        return pltpu.make_async_copy(
-            stage.at[side, span], outs[side].at[span], store_sem.at[side, t]
-        )
-
-    def finish(t):
-        span = pl.ds(pl.multiple_of(t * TILE, TILE), TILE)
-        for side in range(2):
-            stage[side, span] = acc[side, span].astype(jnp.bfloat16)
-            store(side, t).start()
-
-    each(tiles, finish)
+        add_pair(core, FAR, c, last)
+
+    each(chunks - 1, far)
+    far(chunks - 1, True)
 
     def sent(c):
         for role in range(6):
             copy(role, c).wait_send()
 
     each(chunks, sent)
-    for side in range(2):
-        each(tiles, functools.partial(lambda side, t: store(side, t).wait(), side))
 
 
 def per_device(sizes, image, sensor, match, sharpness, shift, gain):
     rows, width = image.shape
     anywhere = pl.BlockSpec(memory_space=pl.ANY)
     scalar = pl.BlockSpec(memory_space=pltpu.SMEM)
-    chunks, tiles = rows // CHUNK, rows // TILE
+    chunks = rows // CHUNK
     return pl.pallas_call(
         functools.partial(kernel, sizes),
-        out_shape=[jax.ShapeDtypeStruct((rows, width), jnp.bfloat16)] * 2,
+        out_shape=[pltpu.VMEM((rows, width), jnp.bfloat16)] * 2,
         in_specs=[anywhere, anywhere, pl.BlockSpec(memory_space=pltpu.VMEM)] + [scalar] * 3,
-        out_specs=[anywhere, anywhere],
+        out_specs=[pl.BlockSpec(memory_space=pltpu.VMEM)] * 2,
         scratch_shapes=[
             pltpu.VMEM((2, rows, width), jnp.bfloat16),
             pltpu.VMEM((6, rows, width), jnp.bfloat16),
             pltpu.VMEM((2, rows, width), jnp.float32),
-            pltpu.VMEM((2, rows, width), jnp.bfloat16),
             pltpu.SemaphoreType.DMA((2,)),
-            pltpu.SemaphoreType.DMA((2, tiles)),
             pltpu.SemaphoreType.DMA((6, chunks)),
             pltpu.SemaphoreType.DMA((6, chunks)),
         ],
         compiler_params=pltpu.CompilerParams(
-            collective_id=0, has_side_effects=True, vmem_limit_bytes=56 * 2**20
+            collective_id=0, has_side_effects=True, vmem_limit_bytes=48 * 2**20
         ),
         cost_estimate=pl.CostEstimate(
             flops=32 * rows * rows * width,

time: 178 us -> 171 us (0.961)
  Pallas kernels: 171 us -> 165 us
    pallas_call x1, Pallas kernels: 171 us -> 165 us  [per_device(): pl.pallas_call(functools.partial(kernel, sizes), out_shape=[pltpu.VMEM((r...]
where the time goes in v3:
time: 171 us
  Pallas kernels  165 us (96%)
  local copies, waits for them, and re-layouts  3.49 us (2%)
  between operations  2.58 us (2%)
    pallas_call x1, Pallas kernels, per_device(): pl.pallas_call(functools.partial(kernel, sizes), out_shape=[pltpu.VMEM((r...  165 us
    unnamed x4, local copies, waits for them, and re-layouts  3.49 us

profile of v3, /device:TPU:0, one launch (start us, length us, event | category | flops | bytes accessed | tf_op | source)
XLA Modules:
  0.0 170.9 jit_solution(13671182044809285107)
XLA Ops:
  2.6 0.0 copy-start
  2.6 0.7 copy-done
  3.3 164.8 %shard_map.77 = (bf16[1024,1152]{1,0:T(8,128)(2,1)S(1)}, bf16[1024,1152]{1,0:T(8,128)(2,1)S(1)}) custom-call(bf16[1024,1152]{1,0:T(8,128)(2,1)} %image_hbm.1, bf16[1024,1152]{1,0:T(8,128)(2,1)} %sensor_hbm.1, s32[1,1024]{1,0:T(1,128)S(1)} %copy-done, f32[1]{0:T(128)S(6)} %copy.12.sharpness_ref, f32[1]{0:T(128)S(6)} %copy.13.shift_ref, f32[1]{0:T(128)S(6)} %copy.14.gain_ref), custom_call_target="tpu_custom_call" | custom-call | flops 38654705664 | bytes 9437184 | tf_op jit(solution)/shard_map/pallas_call | solution.py:195
  168.1 1.4 copy.10
  169.5 1.4 copy.11
Async XLA Ops:
  2.6 0.7 copy-start
